TPU v7x, 512 devices: a whole 4x4x16 slice. The times are simulated.
512 devices in a mesh: dp: 8 (over y_lo, x), shard: 64 (over z, y_hi, core).
Axes of the slice: x: 4, y: 4 (y_hi: 2, y_lo: 2; y = y_hi * 2 + y_lo), z: 16, core: 2. Of those that a mesh axis runs over, the one named last changes fastest.
Arguments:
- edge_feats: bfloat16 [65536, 1024], P(('dp', 'shard')), may hold values from -6 to 6
- edge_dst: int32 [65536], P(('dp', 'shard')), may hold values from 0 to 127
- edge_live: int32 [512], P(('dp', 'shard')), may hold values from 64 to 128, as said below
- coefficients: float32 [128, 32], P('dp'), may hold values from 0.01 to 0.5
- expert_weights: float32 [32, 524288], P(None, 'shard'), may hold values from -0.1875 to 0.1875
- node_cot: bfloat16 [65536, 1024], P(('dp', 'shard')), may hold values from -6 to 6
Outputs:
- node_out: bfloat16 [65536, 1024], P(('dp', 'shard'))
- edge_grad: bfloat16 [65536, 1024], P(('dp', 'shard'))
- weight_grad: float32 [32, 524288], P(None, 'shard')
- coef_grad: float32 [128, 32], P('dp')
Inputs may be any that keep to these rules, and one draw needn't show every extreme that they name: On each device the first edge_live slots of its 128 edge slots are live and the rest are padding; some device has all 128 slots live in every draw.
All inputs are finite; a program needn't handle non-finite values.
Results may differ from a plain program's by a relative error of at most 0.0062.
Values may be sent and summed in bfloat16 or wider, within the bound.
A program may use at most 64 MiB of HBM per device.

v0:
```python
import jax
import jax.numpy as jnp
from jax import lax
from jax.sharding import PartitionSpec as P

DEV_CRYS = 4


def complex_block(flattened, order_size):
    square = order_size * order_size
    real_part = flattened[:square].reshape(order_size, order_size)
    imag_part = flattened[square:].reshape(order_size, order_size)
    upper_half = jnp.concatenate([real_part, imag_part], axis=1)
    lower_half = jnp.concatenate([-imag_part, real_part], axis=1)
    return jnp.concatenate([upper_half, lower_half], axis=0)


def per_device(edge_feats, edge_dst, edge_live, coefficients, expert_weights, node_cot):
    groups = coefficients.shape[0]
    segment = expert_weights.shape[1]
    edge_slots = edge_feats.shape[0]
    atom_count = node_cot.shape[0]
    order_size = edge_feats.shape[1] // 2
    copies = lax.optimization_barrier(expert_weights.astype(jnp.bfloat16)).astype(jnp.float32)
    merged = jnp.dot(coefficients, copies, precision=lax.Precision.HIGHEST).astype(jnp.bfloat16)
    outgoing = jnp.repeat(merged, DEV_CRYS, axis=0)
    incoming = lax.all_to_all(outgoing, "shard", split_axis=0, concat_axis=0, tiled=True)
    flattened = incoming.reshape(-1)
    block_matrix = complex_block(flattened, order_size)
    kept_slots = lax.broadcasted_iota(jnp.int32, (edge_slots,), 0) < edge_live[0]
    atom_index = lax.broadcasted_iota(jnp.int32, (atom_count, edge_slots), 0)
    selector = ((edge_dst[None, :] == atom_index) & kept_slots[None, :]).astype(jnp.bfloat16)
    messages = jnp.dot(edge_feats, block_matrix, preferred_element_type=jnp.float32)
    messages = jnp.where(kept_slots[:, None], messages, 0.0).astype(jnp.bfloat16)
    node_out = jnp.dot(selector, messages, preferred_element_type=jnp.float32).astype(jnp.bfloat16)
    edge_cot = lax.dot_general(
        selector, node_cot, (((0,), (0,)), ((), ())), preferred_element_type=jnp.float32
    ).astype(jnp.bfloat16)
    edge_grad = lax.dot_general(
        edge_cot, block_matrix, (((1,), (1,)), ((), ())), preferred_element_type=jnp.float32
    ).astype(jnp.bfloat16)
    outer = lax.dot_general(
        edge_feats, edge_cot, (((0,), (0,)), ((), ())), preferred_element_type=jnp.float32
    )
    real_grad = outer[:order_size, :order_size] + outer[order_size:, order_size:]
    imag_grad = outer[:order_size, order_size:] - outer[order_size:, :order_size]
    gradient = jnp.concatenate([real_grad.reshape(-1), imag_grad.reshape(-1)]) / edge_slots
    incoming = lax.all_to_all(
        gradient.reshape(-1, segment), "shard", split_axis=0, concat_axis=0, tiled=True
    )
    summed = jnp.sum(incoming.reshape(groups, DEV_CRYS, segment), axis=1)
    group_grad = lax.dot_general(
        coefficients, summed, (((0,), (0,)), ((), ())), precision=lax.Precision.HIGHEST
    )
    weight_grad = lax.psum(group_grad, "dp")
    coef_part = lax.dot_general(
        summed, copies, (((1,), (1,)), ((), ())), precision=lax.Precision.HIGHEST
    )
    coef_grad = lax.psum(coef_part, "shard")
    return (node_out, edge_grad, weight_grad, coef_grad)


def solution(mesh):
    in_specs = (
        P(("dp", "shard"), None),
        P(("dp", "shard")),
        P(("dp", "shard")),
        P("dp", None),
        P(None, "shard"),
        P(("dp", "shard"), None),
    )
    out_specs = (
        P(("dp", "shard"), None),
        P(("dp", "shard"), None),
        P(None, "shard"),
        P("dp", None),
    )
    return jax.shard_map(
        per_device, mesh=mesh, in_specs=in_specs, out_specs=out_specs, check_vma=False
    )
```

profile of v0, /device:TPU:1, one launch (start us, length us, event | category | flops | bytes accessed | tf_op | source)
XLA Modules:
  0.0 380.2 jit_solution(15175295256759752045)
XLA Ops:
  7.2 1.3 convert_element_type.21
  8.5 1.1 convolution_convert_fusion
  9.6 1.4 broadcast_in_dim.19
  11.0 4.6 %all_to_all.13 = bf16[64,1,8192]{2,1,0:T(2,128)(2,1)S(1)} reshape(bf16[16,4,8192]{2,1,0:T(4,128)(2,1)} %broadcast_in_dim.19) | data formatting | bytes 2097152 | tf_op jit(solution)/shard_map/all_to_all | solution.py:27
  16.1 8.1 %reduce.5 = bf16[64,8192]{1,0:T(8,128)(2,1)} reduce(bf16[64,1,8192]{2,1,0:T(2,128)(2,1)S(1)} %all_to_all.13, bf16[]{:T(256)} %broadcast.24), dimensions={1}, to_apply=%all_to_all.13.reduce_sub_computation | reduce | bytes 2097154 | tf_op jit(solution)/shard_map/all_to_all | solution.py:27
  24.2 2.7 reshape.86
  26.9 19.8 %all-to-all-start = ((bf16[64,2,4096]{2,1,0:T(2,128)(2,1)}), bf16[64,2,4096]{2,1,0:T(2,128)(2,1)S(1)}, u32[]{:S(2)}, u32[]{:S(2)}) async-start(bf16[64,2,4096]{2,1,0:T(2,128)(2,1)} %reshape.86), calls=%async_computation | async-start | bytes 2097152 | tf_op jit(solution)/shard_map/all_to_all | solution.py:27
  47.7 0.7 copy-done.3
  48.4 0.7 convolution_bitcast_fusion.1
  49.1 1.9 slice_add_fusion
  50.9 1.6 copy.16
  52.5 1.2 concatenate.27
  53.7 1.6 copy.17
  55.2 1.2 concatenate.28
  56.4 1.7 maximum_multiply_fusion
  58.1 3.5 copy.18
  61.6 39.2 %all-to-all-done = bf16[64,2,4096]{2,1,0:T(2,128)(2,1)S(1)} async-done(((bf16[64,2,4096]{2,1,0:T(2,128)(2,1)}), bf16[64,2,4096]{2,1,0:T(2,128)(2,1)S(1)}, u32[]{:S(2)}, u32[]{:S(2)}) %all-to-all-start) | async-done | bytes 1048608 | tf_op jit(solution)/shard_map/all_to_all | solution.py:27
  100.7 1.0 copy-done.1
  101.7 7.6 %all-to-all-start.1 = ((f32[64,1,8192]{2,1,0:T(1,128)}), f32[64,1,8192]{2,1,0:T(1,128)}, u32[]{:S(2)}, u32[]{:S(2)}) async-start(f32[64,1,8192]{2,1,0:T(1,128)} %copy.18), calls=%async_computation.1 | async-start | bytes 4194304 | tf_op jit(solution)/shard_map/all_to_all | solution.py:48
  109.6 6.5 %reshape.87 = bf16[64,1,8192]{2,1,0:T(2,128)(2,1)S(1)} reshape(bf16[64,2,4096]{2,1,0:T(2,128)(2,1)} %copy-done.1) | data formatting | bytes 2097152
  116.1 91.5 %all-to-all-done.1 = f32[64,1,8192]{2,1,0:T(1,128)} async-done(((f32[64,1,8192]{2,1,0:T(1,128)}), f32[64,1,8192]{2,1,0:T(1,128)}, u32[]{:S(2)}, u32[]{:S(2)}) %all-to-all-start.1) | async-done | bytes 2097184 | tf_op jit(solution)/shard_map/all_to_all | solution.py:48
  207.5 8.2 %reduce.2 = f32[64,8192]{1,0:T(8,128)} reduce(f32[64,1,8192]{2,1,0:T(1,128)} %all-to-all-done.1, f32[]{:T(128)} %constant.11), dimensions={1}, to_apply=%all_to_all.12.reduce_sub_computation | reduce | bytes 4194308 | tf_op jit(solution)/shard_map/all_to_all | solution.py:48
  215.7 2.9 reshape.82
  218.6 2.9 reduce_sum.9
  221.5 2.0 convolution_bitcast_fusion
  223.5 5.8 %slice_reduce_fusion = (bf16[32,8192]{1,0:T(8,128)(2,1)}, bf16[32,8192]{1,0:T(8,128)(2,1)}) fusion(bf16[64,1,8192]{2,1,0:T(2,128)(2,1)S(1)} %reshape.87), kind=kLoop, calls=%fused_computation.12 | loop fusion | bytes 2097152 | tf_op jit(solution)/shard_map/slice | solution.py:12
  229.3 1.4 reshape.81
  230.8 1.1 reshape.80
  231.8 2.8 convolution_convert_fusion.1
  234.6 1.6 convolution_convert_fusion.3
  236.8 134.3 %psum.15 = f32[16,32]{1,0:T(8,128)} all-reduce(f32[16,32]{1,0:T(8,128)S(1)} %fusion.14), channel_id=1, replica_groups=mesh['dp'=8,'shard'=64] {'shard'}, use_global_device_ids=true, to_apply=%region_2.3 | all-reduce | flops 512 | bytes 4096 | tf_op jit(solution)/shard_map/psum | solution.py:59
  371.1 2.3 copy.22
  (24 shorter events, 1.7 us)
Async XLA Ops:
  7.2 41.2 %copy-start = (bf16[128,1024]{1,0:T(8,128)(2,1)S(1)}, bf16[128,1024]{1,0:T(8,128)(2,1)}, u32[]{:S(2)}) copy-start(bf16[128,1024]{1,0:T(8,128)(2,1)} %param.6) | copy-start | bytes 786436
  24.2 23.1 %copy-start.6 = (bf16[128,1024]{1,0:T(8,128)(2,1)S(1)}, bf16[128,1024]{1,0:T(8,128)(2,1)}, u32[]{:S(2)}) copy-start(bf16[128,1024]{1,0:T(8,128)(2,1)} %param.11) | copy-start | bytes 786436
  24.2 23.1 %copy-start.8 = (s32[128]{0:T(128)S(1)}, s32[128]{0:T(128)}, u32[]{:S(2)}) copy-start(s32[128]{0:T(128)} %param.7) | copy-start | bytes 1540
  26.9 73.8 %all-to-all-start = ((bf16[64,2,4096]{2,1,0:T(2,128)(2,1)}), bf16[64,2,4096]{2,1,0:T(2,128)(2,1)S(1)}, u32[]{:S(2)}, u32[]{:S(2)}) async-start(bf16[64,2,4096]{2,1,0:T(2,128)(2,1)} %reshape.86), calls=%async_computation | async-start | bytes 2097152 | tf_op jit(solution)/shard_map/all_to_all | solution.py:27
  47.7 0.7 copy-start.3
  100.7 1.0 copy-start.1
  101.7 105.8 %all-to-all-start.1 = ((f32[64,1,8192]{2,1,0:T(1,128)}), f32[64,1,8192]{2,1,0:T(1,128)}, u32[]{:S(2)}, u32[]{:S(2)}) async-start(f32[64,1,8192]{2,1,0:T(1,128)} %copy.18), calls=%async_computation.1 | async-start | bytes 4194304 | tf_op jit(solution)/shard_map/all_to_all | solution.py:48
  109.3 261.8 %all-reduce.2.cloned.1.call-start = ((), (), s32[]{:S(2)}) async-start(), calls=%async_computation.2 | async-start | bytes 2097152 | tf_op jit(solution)/shard_map/psum | solution.py:55
  218.6 2.9 copy-start.7
  229.3 1.5 copy-start.2
  229.3 2.5 copy-start.4
  231.8 2.8 copy-start.5
Sparse Core Ops, SparseCore 0:
  223.6 81.4 all-reduce.1
where the time goes:
time: 381 us; the launch traced here: 380 us
  blocking collectives  134 us (35%)
  waiting for transfers between devices  131 us (34%)
  local copies, waits for them, and re-layouts  39.6 us (10%)
  starting transfers between devices  27.6 us (7%)
  other arithmetic  24.1 us (6%)
  between operations  14.8 us (4%)
  matrix products  8.98 us (2%)
    psum x1, blocking collectives, per_device(): coef_grad = lax.psum(coef_part, 'shard')  134 us
    all_to_all x1, waiting for transfers between devices, per_device(): lax.all_to_all(gradient.reshape(-1, segment), 'shard', split_axis=0, conc...  91.5 us
    all_to_all x1, waiting for transfers between devices, per_device(): lax.all_to_all(outgoing, 'shard', split_axis=0, concat_axis=0, tiled=True)  39.2 us
    all_to_all x1, starting transfers between devices, per_device(): lax.all_to_all(outgoing, 'shard', split_axis=0, concat_axis=0, tiled=True)  19.8 us
    unnamed x21, local copies, waits for them, and re-layouts  13.1 us
    all_to_all x1, other arithmetic, per_device(): lax.all_to_all(gradient.reshape(-1, segment), 'shard', split_axis=0, conc...  8.19 us
    all_to_all x1, other arithmetic, per_device(): lax.all_to_all(outgoing, 'shard', split_axis=0, concat_axis=0, tiled=True)  8.13 us
  transfers between devices with their start and end apart: 3, of which 2 were waited for; matrix products, arithmetic and copies ran while one was open for 9% of the time, Pallas kernels for 0%

commit v1 on v0

v1 whole, which is shorter than its diff:
```python
import jax
import jax.numpy as jnp
from jax import lax
from jax.experimental import pallas as pl
from jax.experimental.pallas import tpu as pltpu
from jax.sharding import PartitionSpec as P

F32, BF16 = jnp.float32, jnp.bfloat16
NZ, NQ, NG = 16, 4, 8
NX = 4
ROWS, COLS = 16, 512
EDGES, WIDTH, EXPERTS = 128, 1024, 32
YC = 4
DMA = pltpu.SemaphoreType.DMA


def three_parts(value):
    high = value.astype(BF16)
    rest = value - high.astype(F32)
    middle = rest.astype(BF16)
    low = (rest - middle.astype(F32)).astype(BF16)
    return high, middle, low


def tn_dot(a, b):
    return lax.dot_general(a, b, (((0,), (0,)), ((), ())), preferred_element_type=F32)


def nt_dot(a, b):
    return lax.dot_general(a, b, (((1,), (1,)), ((), ())), preferred_element_type=F32)


def kernel(
    feats_in, dst_in, live_in, coef_in, weights_in, cot_in,
    node_out, edge_grad, weight_out, coef_out,
    weights, copies, merged_rows, merged_send, block, feats, node_cot, edge_cot,
    grads, y_send, y_recv, dp_send, dp_recv, z_send, z_recv, crystals, gather,
    gather_send, coef_all, coef_rows, part, part_send, part_recv, sum_send, sum_recv, last,
    in_sem, fz_s, fz_r, fy_s, fy_r, fc_s, fc_r, gc_s, gc_r, ex_s, ex_r, co_s, co_r,
    ys_s, ys_r, da_s, da_r, bz_s, bz_r, ag_s, ag_r, cd_s, cd_r, cz_s, cz_r, cl_s, cl_r,
):
    g = lax.axis_index("dp")
    s = lax.axis_index("shard")
    z = s // NQ
    q = s % NQ
    yh = q // 2
    core = q % 2
    h = g // NX
    x = g % NX
    core_peer = z * NQ + yh * 2 + (1 - core)
    y_peer = z * NQ + (1 - yh) * 2 + core

    def shard_copy(src, dst, send, recv, peer):
        return pltpu.make_async_remote_copy(
            src_ref=src, dst_ref=dst, send_sem=send, recv_sem=recv,
            device_id={"dp": g, "shard": peer}, device_id_type=pl.DeviceIdType.MESH,
        )

    def dp_copy(src, dst, send, recv, peer):
        return pltpu.make_async_remote_copy(
            src_ref=src, dst_ref=dst, send_sem=send, recv_sem=recv,
            device_id={"dp": peer, "shard": s}, device_id_type=pl.DeviceIdType.MESH,
        )

    load_w = pltpu.make_async_copy(weights_in, weights, in_sem.at[0])
    load_f = pltpu.make_async_copy(feats_in, feats.at[0], in_sem.at[1])
    load_c = pltpu.make_async_copy(cot_in, node_cot, in_sem.at[2])
    load_w.start()
    load_f.start()
    load_c.start()

    barrier = pltpu.get_barrier_semaphore()

    def greet_shard(peer):
        pl.semaphore_signal(
            barrier, inc=1, device_id={"dp": g, "shard": peer}, device_id_type=pl.DeviceIdType.MESH
        )

    greet_shard(core_peer)
    greet_shard(y_peer)

    @pl.loop(1, NZ)
    def _(off):
        greet_shard(((z + off) % NZ) * NQ + q)

    @pl.loop(1, NG)
    def _(off):
        pl.semaphore_signal(
            barrier, inc=1, device_id={"dp": (g + off) % NG, "shard": s}, device_id_type=pl.DeviceIdType.MESH
        )

    coef = coef_in[...]
    stacked = jnp.concatenate(three_parts(coef), axis=0)
    coef_all[g] = jnp.concatenate([coef, jnp.zeros((NZ, 128 - EXPERTS), F32)], axis=1)
    load_w.wait()
    for row in range(ROWS):
        lanes = pl.ds(row * COLS, COLS)
        rounded = weights[:, lanes].astype(BF16)
        copies[:, lanes] = rounded
        terms = jnp.dot(stacked, rounded, preferred_element_type=F32)
        merged_rows[:, row, :] = terms[0:NZ] + terms[NZ : 2 * NZ] + terms[2 * NZ : 3 * NZ]
    merged_send[...] = merged_rows[...].astype(BF16)

    pl.semaphore_wait(barrier, 2 + (NZ - 1) + (NG - 1))

    def fz(off):
        to = (z + off) % NZ
        return shard_copy(merged_send.at[to], block.at[z, q], fz_s.at[off], fz_r.at[off], to * NQ + q)

    def fz_in(off):
        at = (z + NZ - off) % NZ
        return shard_copy(merged_send.at[at], block.at[at, q], fz_s.at[off], fz_r.at[off], at * NQ + q)

    @pl.loop(1, NZ)
    def _(off):
        fz(off).start()

    block[z, q] = merged_send[z]

    load_f.wait()
    feats_copy = shard_copy(feats.at[0], feats.at[1], ex_s.at[0], ex_r.at[0], core_peer)
    feats_copy.start()
    atom = lax.broadcasted_iota(jnp.int32, (EDGES, EDGES), 0)
    slot = lax.broadcasted_iota(jnp.int32, (EDGES, EDGES), 1)
    chosen = (dst_in[...] == atom) & (slot < live_in[0])
    selector = jnp.where(chosen, 1.0, 0.0).astype(BF16)
    load_c.wait()
    edge_cot[0] = tn_dot(selector, node_cot[...]).astype(BF16)
    cot_copy = shard_copy(edge_cot.at[0], edge_cot.at[1], ex_s.at[1], ex_r.at[1], core_peer)
    cot_copy.start()

    def co(off):
        to = (g + off) % NG
        return dp_copy(coef_all.at[g], coef_all.at[g], co_s.at[off], co_r.at[off], to)

    def co_in(off):
        at = (g + NG - off) % NG
        return dp_copy(coef_all.at[at], coef_all.at[at], co_s.at[off], co_r.at[off], at)

    @pl.loop(1, NG)
    def _(off):
        co(off).start()

    feats_copy.wait_recv()
    cot_copy.wait_recv()
    half = WIDTH // 2
    left, right = [], []
    for device in range(2):
        f, c = feats[device], edge_cot[device]
        left += [f[:, :half], f[:, half:]]
        right += [
            jnp.concatenate([c[:, :half], c[:, half:]], axis=1),
            jnp.concatenate([c[:, half:], -c[:, :half]], axis=1),
        ]
    outer = tn_dot(jnp.concatenate(left, axis=0), jnp.concatenate(right, axis=0)) * (1.0 / EDGES)
    grads[0 : NZ // 2] = outer[:, :half].reshape(NZ // 2, 2, 2, ROWS, COLS)
    grads[NZ // 2 : NZ] = outer[:, half:].reshape(NZ // 2, 2, 2, ROWS, COLS)
    y_send[...] = grads[:, 1 - yh, core].astype(BF16)

    per = NZ // YC

    def ys(chunk):
        at = pl.ds(chunk * per, per)
        return shard_copy(y_send.at[at], y_recv.at[at], ys_s.at[chunk], ys_r.at[chunk], y_peer)

    for chunk in range(YC):
        ys(chunk).start()

    def fy(off):
        at = (z + NZ - off) % NZ
        return shard_copy(block.at[at, q], block.at[at, q], fy_s.at[off], fy_r.at[off], y_peer)

    def fc(off):
        at = (z + NZ - off) % NZ
        return shard_copy(block.at[at, q], block.at[at, q], fc_s.at[off], fc_r.at[off], core_peer)

    q_y = (1 - yh) * 2 + core
    q_c = yh * 2 + (1 - core)
    q_yc = (1 - yh) * 2 + (1 - core)

    def fy_in(off):
        at = (z + NZ - off) % NZ
        return shard_copy(block.at[at, q_y], block.at[at, q_y], fy_s.at[off], fy_r.at[off], y_peer)

    def fc_in(off):
        at = (z + NZ - off) % NZ
        return shard_copy(block.at[at, q_c], block.at[at, q_c], fc_s.at[off], fc_r.at[off], core_peer)

    def gc(off):
        at = (z + NZ - off) % NZ
        return shard_copy(block.at[at, q_y], block.at[at, q_y], gc_s.at[off], gc_r.at[off], core_peer)

    def gc_in(off):
        at = (z + NZ - off) % NZ
        return shard_copy(block.at[at, q_yc], block.at[at, q_yc], gc_s.at[off], gc_r.at[off], core_peer)

    fy(0).start()
    fc(0).start()

    def forward(low, high):
        @pl.loop(low, high)
        def _(step):
            for off in (step, NZ - step):
                fz_in(off).wait_recv()
                fy(off).start()
                fc(off).start()

    forward(1, 4)

    for chunk in range(YC):
        ys(chunk).wait_recv()
    for p in range(NZ // 2):
        low = grads[p, yh, core] + y_recv[p].astype(F32)
        high = grads[p + NZ // 2, yh, core] + y_recv[p + NZ // 2].astype(F32)
        for to in range(NG):
            rows = slice((to // NX) * 8, (to // NX) * 8 + 8)
            lanes = slice((to % NX) * 128, (to % NX) * 128 + 128)
            dp_send[to, p] = jnp.concatenate([low[rows, lanes], high[rows, lanes]], axis=0).astype(BF16)

    def da(off):
        to = (g + off) % NG
        return dp_copy(dp_send.at[to], dp_recv.at[g], da_s.at[off], da_r.at[off], to)

    def da_in(off):
        at = (g + NG - off) % NG
        return dp_copy(dp_send.at[at], dp_recv.at[at], da_s.at[off], da_r.at[off], at)

    @pl.loop(1, NG)
    def _(off):
        da(off).start()

    dp_recv[g] = dp_send[g]

    forward(4, 8)
    fz_in(8).wait_recv()
    fy(8).start()
    fc(8).start()

    @pl.loop(1, NG)
    def _(off):
        da_in(off).wait_recv()

    for p in range(NZ // 2):
        for j in range(NG // 2):
            even = dp_recv[2 * j, p].astype(F32)
            odd = dp_recv[2 * j + 1, p].astype(F32)
            z_send[p, j] = jnp.concatenate([even[:8], odd[:8]], axis=0).astype(BF16)
            z_send[p + NZ // 2, j] = jnp.concatenate([even[8:], odd[8:]], axis=0).astype(BF16)

    def bz(off):
        to = (z + off) % NZ
        return shard_copy(z_send.at[to], z_recv.at[z], bz_s.at[off], bz_r.at[off], to * NQ + q)

    def bz_in(off):
        at = (z + NZ - off) % NZ
        return shard_copy(z_send.at[at], z_recv.at[at], bz_s.at[off], bz_r.at[off], at * NQ + q)

    @pl.loop(1, NZ)
    def _(off):
        bz(off).start()

    z_recv[z] = z_send[z]

    @pl.loop(0, NZ)
    def _(off):
        fy_in(off).wait_recv()
        gc(off).start()

    @pl.loop(0, NZ)
    def _(off):
        fc_in(off).wait_recv()
        gc_in(off).wait_recv()

    matrix = block[...].reshape(NZ * NQ * ROWS, COLS)
    f = feats[0]
    lifted = jnp.concatenate(
        [
            jnp.concatenate([f[:, :half], -f[:, half:]], axis=1),
            jnp.concatenate([f[:, half:], f[:, :half]], axis=1),
        ],
        axis=0,
    )
    messages = jnp.dot(lifted, matrix, preferred_element_type=F32).astype(BF16)
    messages = jnp.concatenate([messages[:EDGES], messages[EDGES:]], axis=1)
    node_out[...] = jnp.dot(selector, messages, preferred_element_type=F32).astype(BF16)
    c = edge_cot[0]
    products = nt_dot(jnp.concatenate([c[:, :half], c[:, half:]], axis=0), matrix)
    edge_grad[:, :half] = (products[:EDGES, :half] + products[EDGES:, half:]).astype(BF16)
    edge_grad[:, half:] = (products[EDGES:, :half] - products[:EDGES, half:]).astype(BF16)

    @pl.loop(1, NG)
    def _(off):
        co_in(off).wait_recv()

    for group in range(NG):
        coef_rows[:, group, :] = coef_all[group]
    all_coef = coef_rows[...].reshape(NZ * NG, 128)[:, :EXPERTS]
    all_parts = jnp.concatenate(three_parts(all_coef), axis=1)

    @pl.loop(1, NZ)
    def _(off):
        bz_in(off).wait_recv()

    crystals[...] = z_recv[...].astype(F32).reshape(NZ * NG, 8, 128)
    flat = jnp.concatenate([crystals[:, row, :] for row in range(8)], axis=1).astype(BF16)
    terms = tn_dot(all_parts, flat)
    total = (terms[:EXPERTS] + terms[EXPERTS : 2 * EXPERTS] + terms[2 * EXPERTS :]).astype(BF16)
    for row in range(8):
        gather_send[row] = total[:, row * 128 : row * 128 + 128]

    def ag(off):
        to = (g + off) % NG
        return dp_copy(gather_send, gather.at[pl.ds(h * 8, 8), x], ag_s.at[off], ag_r.at[off], to)

    def ag_in(off):
        at = (g + NG - off) % NG
        return dp_copy(gather_send, gather.at[pl.ds((at // NX) * 8, 8), at % NX], ag_s.at[off], ag_r.at[off], at)

    @pl.loop(1, NG)
    def _(off):
        ag(off).start()

    gather[pl.ds(h * 8, 8), x] = gather_send[...]

    own = jnp.concatenate(
        [
            copies[:, pl.ds(pl.multiple_of((h * 8 + row) * COLS + x * 128, 128), 128)]
            for row in range(8)
        ],
        axis=1,
    )
    total_part = jnp.zeros((4 * NG, 128), F32)
    zero = jnp.zeros_like(own)
    for b in range(4):
        rows = jnp.concatenate(
            [flat[(4 * a + b) * NG : (4 * a + b) * NG + NG] for a in range(4)], axis=0
        )
        placed = jnp.concatenate([own if k == b else zero for k in range(4)], axis=0)
        total_part = total_part + nt_dot(rows, placed)
    part[...] = total_part.reshape(4, NG, 128)
    empty = jnp.zeros((4, 128), F32)
    for group in range(NG):
        part_send[group] = jnp.concatenate([part[:, group, :], empty], axis=0)

    def cd(off):
        to = (g + off) % NG
        return dp_copy(part_send.at[to], part_recv.at[g], cd_s.at[off], cd_r.at[off], to)

    def cd_in(off):
        at = (g + NG - off) % NG
        return dp_copy(part_send.at[at], part_recv.at[at], cd_s.at[off], cd_r.at[off], at)

    @pl.loop(1, NG)
    def _(off):
        cd(off).start()

    part_recv[g] = part_send[g]

    @pl.loop(1, NG)
    def _(off):
        cd_in(off).wait_recv()

    sum_send[...] = jnp.sum(part_recv[...], axis=0)

    def cz(off):
        to = (z + off) % NZ
        return shard_copy(sum_send, sum_recv.at[z], cz_s.at[off], cz_r.at[off], to * NQ + q)

    def cz_in(off):
        at = (z + NZ - off) % NZ
        return shard_copy(sum_send, sum_recv.at[at], cz_s.at[off], cz_r.at[off], at * NQ + q)

    @pl.loop(1, NZ)
    def _(off):
        cz(off).start()

    sum_recv[z] = sum_send[...]

    @pl.loop(1, NZ)
    def _(off):
        cz_in(off).wait_recv()

    last[0] = jnp.sum(sum_recv[...], axis=0)
    core_copy = shard_copy(last.at[0], last.at[1], cl_s.at[0], cl_r.at[0], core_peer)
    core_copy.start()
    core_copy.wait_recv()
    last[2] = last[0] + last[1]
    y_copy = shard_copy(last.at[2], last.at[3], cl_s.at[1], cl_r.at[1], y_peer)
    y_copy.start()
    y_copy.wait_recv()
    summed = (last[2] + last[3])[:4]
    coef_out[...] = jnp.concatenate(
        [summed[a : a + 1, b * EXPERTS : (b + 1) * EXPERTS] for a in range(4) for b in range(4)], axis=0
    )

    @pl.loop(1, NG)
    def _(off):
        ag_in(off).wait_recv()

    for row in range(ROWS):
        for tile in range(NX):
            weight_out[:, pl.ds((row * NX + tile) * 128, 128)] = gather[row, tile]

    @pl.loop(1, NZ)
    def _(off):
        fz(off).wait_send()
        bz(off).wait_send()
        cz(off).wait_send()

    @pl.loop(0, NZ)
    def _(off):
        fy(off).wait_send()
        fc(off).wait_send()
        gc(off).wait_send()

    @pl.loop(1, NG)
    def _(off):
        co(off).wait_send()
        da(off).wait_send()
        ag(off).wait_send()
        cd(off).wait_send()

    feats_copy.wait_send()
    cot_copy.wait_send()
    core_copy.wait_send()
    y_copy.wait_send()
    for chunk in range(YC):
        ys(chunk).wait_send()


def per_device(edge_feats, edge_dst, edge_live, coefficients, expert_weights, node_cot):
    vmem = pl.BlockSpec(memory_space=pltpu.VMEM)
    smem = pl.BlockSpec(memory_space=pltpu.SMEM)
    hbm = pl.BlockSpec(memory_space=pl.ANY)
    node_out, edge_grad, weight_grad, coef_grad = pl.pallas_call(
        kernel,
        out_shape=(
            jax.ShapeDtypeStruct((EDGES, WIDTH), BF16),
            jax.ShapeDtypeStruct((EDGES, WIDTH), BF16),
            jax.ShapeDtypeStruct((EXPERTS, ROWS * COLS), BF16),
            jax.ShapeDtypeStruct((NZ, EXPERTS), F32),
        ),
        in_specs=[hbm, vmem, smem, vmem, hbm, hbm],
        out_specs=(vmem, vmem, vmem, vmem),
        scratch_shapes=[
            pltpu.VMEM((EXPERTS, ROWS * COLS), F32),
            pltpu.VMEM((EXPERTS, ROWS * COLS), BF16),
            pltpu.VMEM((NZ, ROWS, COLS), F32),
            pltpu.VMEM((NZ, ROWS, COLS), BF16),
            pltpu.VMEM((NZ, NQ, ROWS, COLS), BF16),
            pltpu.VMEM((2, EDGES, WIDTH), BF16),
            pltpu.VMEM((EDGES, WIDTH), BF16),
            pltpu.VMEM((2, EDGES, WIDTH), BF16),
            pltpu.VMEM((NZ, 2, 2, ROWS, COLS), F32),
            pltpu.VMEM((NZ, ROWS, COLS), BF16),
            pltpu.VMEM((NZ, ROWS, COLS), BF16),
            pltpu.VMEM((NG, NZ // 2, 16, 128), BF16),
            pltpu.VMEM((NG, NZ // 2, 16, 128), BF16),
            pltpu.VMEM((NZ, NG // 2, 16, 128), BF16),
            pltpu.VMEM((NZ, NG // 2, 16, 128), BF16),
            pltpu.VMEM((NZ * NG, 8, 128), F32),
            pltpu.VMEM((ROWS, NX, EXPERTS, 128), BF16),
            pltpu.VMEM((8, EXPERTS, 128), BF16),
            pltpu.VMEM((NG, NZ, 128), F32),
            pltpu.VMEM((NZ, NG, 128), F32),
            pltpu.VMEM((4, NG, 128), F32),
            pltpu.VMEM((NG, 8, 128), F32),
            pltpu.VMEM((NG, 8, 128), F32),
            pltpu.VMEM((8, 128), F32),
            pltpu.VMEM((NZ, 8, 128), F32),
            pltpu.VMEM((4, 8, 128), F32),
            DMA((3,)),
            DMA((NZ,)), DMA((NZ,)), DMA((NZ,)), DMA((NZ,)), DMA((NZ,)), DMA((NZ,)), DMA((NZ,)), DMA((NZ,)),
            DMA((2,)), DMA((2,)), DMA((NG,)), DMA((NG,)),
            DMA((YC,)), DMA((YC,)), DMA((NG,)), DMA((NG,)), DMA((NZ,)), DMA((NZ,)),
            DMA((NG,)), DMA((NG,)), DMA((NG,)), DMA((NG,)), DMA((NZ,)), DMA((NZ,)), DMA((2,)), DMA((2,)),
        ],
        compiler_params=pltpu.CompilerParams(
            collective_id=0, has_side_effects=True, vmem_limit_bytes=40 * 1024 * 1024
        ),
    )(edge_feats, edge_dst.reshape(1, EDGES), edge_live, coefficients, expert_weights, node_cot)
    return node_out, edge_grad, weight_grad.astype(F32), coef_grad


def solution(mesh):
    in_specs = (
        P(("dp", "shard"), None),
        P(("dp", "shard")),
        P(("dp", "shard")),
        P("dp", None),
        P(None, "shard"),
        P(("dp", "shard"), None),
    )
    out_specs = (
        P(("dp", "shard"), None),
        P(("dp", "shard"), None),
        P(None, "shard"),
        P("dp", None),
    )
    return jax.shard_map(
        per_device, mesh=mesh, in_specs=in_specs, out_specs=out_specs, check_vma=False
    )
```

time: 381 us -> 81.9 us (0.21)
  blocking collectives: 134 us -> 0 us
  waiting for transfers between devices: 131 us -> 0 us
  Pallas kernels: 0 us -> 72.9 us
  local copies, waits for them, and re-layouts: 39.6 us -> 6.47 us
  starting transfers between devices: 27.6 us -> 0 us
  other arithmetic: 24.1 us -> 1.04 us
  between operations: 14.8 us -> 1.3 us
  matrix products: 8.98 us -> 0 us
    psum x1 -> x0, blocking collectives: 134 us -> none  [per_device(): coef_grad = lax.psum(coef_part, 'shard')]
    all_to_all x2 -> x0, waiting for transfers between devices: 131 us -> none  [the longest x1 91.5 us: per_device(): lax.all_to_all(gradient.reshape(-1, segment), 'shard', split_axis=0, conc...]
    pallas_call x0 -> x1, Pallas kernels: none -> 72.9 us  [per_device(): pl.pallas_call(kernel, out_shape=(jax.ShapeDtypeStruct((EDGES, WIDTH), BF...]
    all_to_all x2 -> x0, starting transfers between devices: 27.4 us -> none  [the longest x1 19.8 us: per_device(): lax.all_to_all(outgoing, 'shard', split_axis=0, concat_axis=0, tiled=True)]
    all_to_all x2 -> x0, other arithmetic: 16.3 us -> none  [the longest x1 8.19 us: per_device(): lax.all_to_all(gradient.reshape(-1, segment), 'shard', split_axis=0, conc...]
    dot_general x7 -> x0, matrix products: 8.98 us -> none  [the longest x1 2.78 us: per_device(): lax.dot_general(edge_cot, block_matrix, (((1,), (1,)), ((), ())), preferr...]
    unnamed x21 -> x13, local copies, waits for them, and re-layouts: 13.1 us -> 6.47 us
    slice x1 -> x0, local copies, waits for them, and re-layouts: 5.78 us -> none  [complex_block(): imag_part = flattened[square:].reshape(order_size, order_size)]
  transfers between devices with their start and end apart: 3 -> 0, of which waited for: 2 -> 0; matrix products, arithmetic and copies ran while one was open for 9% -> 0% of each run, Pallas kernels for 0% -> 0%
where the time goes in v1:
time: 81.9 us; the launch traced here: 81.7 us
  Pallas kernels  72.9 us (89%)
  local copies, waits for them, and re-layouts  6.47 us (8%)
  between operations  1.3 us (2%)
  other arithmetic  1.04 us (1%)
    pallas_call x1, Pallas kernels, per_device(): pl.pallas_call(kernel, out_shape=(jax.ShapeDtypeStruct((EDGES, WIDTH), BF...  72.9 us
    unnamed x13, local copies, waits for them, and re-layouts  6.47 us

profile of v1, /device:TPU:1, one launch (start us, length us, event | category | flops | bytes accessed | tf_op | source)
XLA Modules:
  0.0 81.7 jit_solution(10319999932447752309)
XLA Ops:
  1.3 0.0 copy-start.4
  1.3 0.6 copy-done.4
  1.9 0.0 copy-start
  1.9 1.2 %copy-done = f32[32,8192]{1,0:T(8,128)S(1)} copy-done((f32[32,8192]{1,0:T(8,128)S(1)}, f32[32,8192]{1,0:T(8,128)}, u32[]{:S(2)}) %copy-start) | copy-done | bytes 1048600
  3.2 0.0 copy-start.1
  3.2 0.9 %copy-done.1 = bf16[128,1024]{1,0:T(8,128)(2,1)S(1)} copy-done((bf16[128,1024]{1,0:T(8,128)(2,1)S(1)}, bf16[128,1024]{1,0:T(8,128)(2,1)}, u32[]{:S(2)}) %copy-start.1) | copy-done | bytes 262168
  4.1 0.0 copy-start.2
  4.1 0.9 %copy-done.2 = bf16[128,1024]{1,0:T(8,128)(2,1)S(1)} copy-done((bf16[128,1024]{1,0:T(8,128)(2,1)S(1)}, bf16[128,1024]{1,0:T(8,128)(2,1)}, u32[]{:S(2)}) %copy-start.2) | copy-done | bytes 262168
  5.1 0.0 copy-start.3
  5.1 0.7 copy-done.3
  5.8 72.9 %shard_map.93 = (bf16[128,1024]{1,0:T(8,128)(2,1)S(1)}, bf16[128,1024]{1,0:T(8,128)(2,1)S(1)}, bf16[32,8192]{1,0:T(8,128)(2,1)S(1)}, f32[16,32]{1,0:T(8,128)S(1)}) custom-call(bf16[128,1024]{1,0:T(8,128)(2,1)S(1)} %copy-done.1, s32[1,128]{1,0:T(1,128)S(1)} %bitcast.1, s32[1]{0:T(128)S(6)} %copy.13.live_in, f32[16,32]{1,0:T(8,128)S(1)} %copy-done.3, ...), custom_call_target="tpu_custom_call" | custom-call | tf_op jit(solution)/shard_map/pallas_call | solution.py:435
  78.6 1.0 %convert_element_type.3 = f32[32,8192]{1,0:T(8,128)} convert(bf16[32,8192]{1,0:T(8,128)(2,1)S(1)} %get-tuple-element.10) | non-fusion elementwise | flops 262144 | bytes 1572864 | tf_op jit(solution)/shard_map/convert_element_type | solution.py:482
  79.7 0.7 copy.14
  80.4 0.7 copy.15
  81.1 0.6 copy.16
Async XLA Ops:
  1.3 0.7 copy-start.4
  1.9 1.2 %copy-start = (f32[32,8192]{1,0:T(8,128)S(1)}, f32[32,8192]{1,0:T(8,128)}, u32[]{:S(2)}) copy-start(f32[32,8192]{1,0:T(8,128)} %weights_in.1) | copy-start | bytes 3145732
  3.2 0.9 %copy-start.1 = (bf16[128,1024]{1,0:T(8,128)(2,1)S(1)}, bf16[128,1024]{1,0:T(8,128)(2,1)}, u32[]{:S(2)}) copy-start(bf16[128,1024]{1,0:T(8,128)(2,1)} %feats_in.1) | copy-start | bytes 786436
  4.1 0.9 %copy-start.2 = (bf16[128,1024]{1,0:T(8,128)(2,1)S(1)}, bf16[128,1024]{1,0:T(8,128)(2,1)}, u32[]{:S(2)}) copy-start(bf16[128,1024]{1,0:T(8,128)(2,1)} %cot_in.1) | copy-start | bytes 786436
  5.1 0.7 copy-start.3

commit v2 on v0

v2 whole, which is shorter than its diff:
```python
import jax
import jax.numpy as jnp
from jax import lax
from jax.experimental import pallas as pl
from jax.experimental.pallas import tpu as pltpu
from jax.sharding import PartitionSpec as P

F32, BF16 = jnp.float32, jnp.bfloat16
NZ, NQ, NG = 16, 4, 8
NX = 4
ROWS, COLS = 16, 512
EDGES, WIDTH, EXPERTS = 128, 1024, 32
YC = 4
PER = NZ // YC
OFFS = [8, 7, 9, 6, 10, 5, 11, 4, 12, 3, 13, 2, 14, 1, 15, 0]
FAR = 5
GROUPS = [[0, 8, 7, 9, 6, 10], [5, 11, 4, 12], [3, 13], [2, 14], [1, 15]]
GROUP_OF = {off: group for group, offs in enumerate(GROUPS) for off in offs}
DMA = pltpu.SemaphoreType.DMA


def three_parts(value):
    high = value.astype(BF16)
    rest = value - high.astype(F32)
    middle = rest.astype(BF16)
    low = (rest - middle.astype(F32)).astype(BF16)
    return high, middle, low


def tn_dot(a, b):
    return lax.dot_general(a, b, (((0,), (0,)), ((), ())), preferred_element_type=F32)


def nt_dot(a, b):
    return lax.dot_general(a, b, (((1,), (1,)), ((), ())), preferred_element_type=F32)


def kernel(
    feats_in, dst_in, live_in, coef_in, weights_in, cot_in,
    node_out, edge_grad, weight_out, coef_out,
    weights, copies, coef, dst, merged_rows, merged_send, block, feats, node_cot, edge_cot,
    grads, y_send, y_recv, z_send, z_recv, z_wide, dp_send, dp_recv, crystals, gather,
    gather_send, coef_all, planes, part, sum_send, sum_recv,
    node_rows, grad_rows, weight_rows,
    in_sem, out_sem, fz_s, fz_r, fy_s, fy_r, fc_s, fc_r, gc_s, gc_r, ex_s, ex_r, co_s, co_r,
    ys_s, ys_r, bz_s, bz_r, da_s, da_r, ag_s, ag_r, cz_s, cz_r, pt_s, pt_r,
):
    g = lax.axis_index("dp")
    s = lax.axis_index("shard")
    z = s // NQ
    q = s % NQ
    yh = q // 2
    core = q % 2
    h = g // NX
    x = g % NX
    q_y = (1 - yh) * 2 + core
    q_c = yh * 2 + (1 - core)
    q_yc = (1 - yh) * 2 + (1 - core)
    core_peer = z * NQ + q_c
    y_peer = z * NQ + q_y
    half = WIDTH // 2

    load_w = pltpu.make_async_copy(weights_in, weights, in_sem.at[0])
    load_f = pltpu.make_async_copy(feats_in, feats.at[0], in_sem.at[1])
    load_c = pltpu.make_async_copy(cot_in, node_cot, in_sem.at[2])
    load_k = pltpu.make_async_copy(coef_in, coef, in_sem.at[3])
    load_d = pltpu.make_async_copy(dst_in, dst, in_sem.at[4])
    for load in (load_w, load_k, load_d, load_c, load_f):
        load.start()

    def copy_to(src, dst, send, recv, dp, shard):
        return pltpu.make_async_remote_copy(
            src_ref=src, dst_ref=dst, send_sem=send, recv_sem=recv,
            device_id={"dp": dp, "shard": shard}, device_id_type=pl.DeviceIdType.MESH,
        )

    def shard_copy(src, dst, send, recv, peer):
        return copy_to(src, dst, send, recv, g, peer)

    def dp_copy(src, dst, send, recv, peer):
        return copy_to(src, dst, send, recv, peer, s)

    def sent(ref, sem):
        shard_copy(ref, ref, sem, sem, core_peer).wait_send()

    def arrived(ref, sem):
        shard_copy(ref, ref, sem, sem, core_peer).wait_recv()

    def ahead(off):
        return (z + off) % NZ

    def behind(off):
        return (z + NZ - off) % NZ

    barrier = pltpu.get_barrier_semaphore()

    def greet(dp, shard):
        pl.semaphore_signal(
            barrier, inc=1, device_id={"dp": dp, "shard": shard}, device_id_type=pl.DeviceIdType.MESH
        )

    for off in OFFS[:-1]:
        greet(g, ahead(off) * NQ + q)
    for off in range(1, NG):
        greet((g + off) % NG, s)
    greet(g, core_peer)
    greet(g, y_peer)

    load_k.wait()
    stacked = jnp.concatenate(three_parts(coef[...]), axis=0)
    blank = jnp.zeros((1, 128 - EXPERTS), F32)
    for j in range(NZ):
        row = coef[pl.ds(behind(OFFS[j]), 1), :]
        coef_all[g, pl.ds(j, 1), :] = jnp.concatenate([row, blank], axis=1)
    load_w.wait()
    for row in range(ROWS):
        lanes = pl.ds(row * COLS, COLS)
        rounded = weights[:, lanes].astype(BF16)
        copies[:, lanes] = rounded
        terms = jnp.dot(stacked, rounded, preferred_element_type=F32)
        merged_rows[:, row, :] = terms[0:NZ] + terms[NZ : 2 * NZ] + terms[2 * NZ : 3 * NZ]
    merged_send[...] = merged_rows[...].astype(BF16)
    block[z, q] = merged_send[z]

    load_d.wait()
    atom = lax.broadcasted_iota(jnp.int32, (EDGES, EDGES), 0)
    slot = lax.broadcasted_iota(jnp.int32, (EDGES, EDGES), 1)
    chosen = (dst[...] == atom) & (slot < live_in[0])
    selector = jnp.where(chosen, 1.0, 0.0).astype(BF16)
    load_c.wait()
    edge_cot[0] = tn_dot(selector, node_cot[...]).astype(BF16)
    load_f.wait()

    pl.semaphore_wait(barrier, 2 + (NZ - 1) + (NG - 1))

    feats_copy = shard_copy(feats.at[0], feats.at[1], ex_s.at[0], ex_r.at[0], core_peer)
    cot_copy = shard_copy(edge_cot.at[0], edge_cot.at[1], ex_s.at[1], ex_r.at[1], core_peer)
    feats_copy.start()
    cot_copy.start()

    def fz(off):
        to = ahead(off)
        return shard_copy(merged_send.at[to], block.at[z, q], fz_s, fz_r.at[GROUP_OF[off]], to * NQ + q)

    for off in OFFS[:FAR]:
        fz(off).start()
    for off in range(1, NG):
        dp_copy(coef_all.at[g], coef_all.at[g], co_s, co_r, (g + off) % NG).start()

    feats_copy.wait_recv()
    cot_copy.wait_recv()
    left, right = [], []
    for device in range(2):
        f, c = feats[device], edge_cot[device]
        left += [f[:, :half], f[:, half:]]
        right += [
            jnp.concatenate([c[:, :half], c[:, half:]], axis=1),
            jnp.concatenate([c[:, half:], -c[:, :half]], axis=1),
        ]
    outer = tn_dot(jnp.concatenate(left, axis=0), jnp.concatenate(right, axis=0)) * (1.0 / EDGES)
    grads[0 : NZ // 2] = outer[:, :half].reshape(NZ // 2, 2, 2, ROWS, COLS)
    grads[NZ // 2 : NZ] = outer[:, half:].reshape(NZ // 2, 2, 2, ROWS, COLS)

    def ys(chunk):
        at = pl.ds(chunk * PER, PER)
        return shard_copy(y_send.at[at], y_recv.at[at], ys_s.at[chunk], ys_r.at[chunk], y_peer)

    for chunk in range(YC):
        for j in range(chunk * PER, chunk * PER + PER):
            y_send[j] = grads[ahead(OFFS[j]), 1 - yh, core].astype(BF16)
        ys(chunk).start()

    for chunk in range(YC):
        ys(chunk).wait_recv()
        for j in range(chunk * PER, chunk * PER + PER):
            to = ahead(OFFS[j])
            z_send[j] = (grads[to, yh, core] + y_recv[j].astype(F32)).astype(BF16)
            if j < NZ - 1:
                shard_copy(z_send.at[j], z_recv.at[j], bz_s, bz_r.at[j // 8], to * NQ + q).start()
    z_recv[NZ - 1] = z_send[NZ - 1]

    for off in OFFS[FAR:-1]:
        fz(off).start()

    def forward(group):
        away = [off for off in GROUPS[group] if off > 0]
        arrived(merged_send.at[pl.ds(0, len(away))], fz_r.at[group])
        for off in GROUPS[group]:
            piece = block.at[behind(off), q]
            shard_copy(piece, piece, fy_s, fy_r.at[group], y_peer).start()
            shard_copy(piece, piece, fc_s, fc_r, core_peer).start()

    def forward_again(group):
        arrived(merged_send.at[pl.ds(0, len(GROUPS[group]))], fy_r.at[group])
        for off in GROUPS[group]:
            piece = block.at[behind(off), q_y]
            shard_copy(piece, piece, gc_s, gc_r, core_peer).start()

    def own_slice(group):
        slots = slice(group * 8, group * 8 + 8)
        wide = z_recv[slots].astype(F32)
        z_wide[slots] = wide
        flat = jnp.concatenate([z_wide[slots, row, :] for row in range(ROWS)], axis=1).astype(BF16)
        found = nt_dot(flat, copies[...])
        for j in range(8):
            planes[pl.ds(behind(OFFS[group * 8 + j]), 1), :] = jnp.concatenate([found[j : j + 1], blank], axis=1)
        for to in range(NG):
            rows = slice((to // NX) * 8, (to // NX) * 8 + 8)
            lanes = slice((to % NX) * 128, (to % NX) * 128 + 128)
            for m in range(4):
                dp_send[group, to, m] = jnp.concatenate(
                    [wide[2 * m, rows, lanes], wide[2 * m + 1, rows, lanes]], axis=0
                ).astype(BF16)
        for off in range(1, NG):
            to = (g + off) % NG
            dp_copy(dp_send.at[group, to], dp_recv.at[group, g], da_s.at[group], da_r.at[group], to).start()
        dp_recv[group, g] = dp_send[group, g]

    forward(0)
    arrived(z_recv.at[pl.ds(0, 8)], bz_r.at[0])
    own_slice(0)
    arrived(z_recv.at[pl.ds(0, 7)], bz_r.at[1])
    own_slice(1)

    part[0] = jnp.concatenate([planes[pl.ds(b, 4, stride=4), :][:, :EXPERTS] for b in range(4)], axis=1)
    core_part = shard_copy(part.at[0], part.at[1], pt_s.at[0], pt_r.at[0], core_peer)
    core_part.start()
    core_part.wait_recv()
    part[2] = part[0] + part[1]
    y_part = shard_copy(part.at[2], part.at[3], pt_s.at[1], pt_r.at[1], y_peer)
    y_part.start()

    for group in range(1, len(GROUPS)):
        forward(group)

    y_part.wait_recv()
    sum_send[...] = part[2] + part[3]
    for off in OFFS[:-1]:
        shard_copy(sum_send, sum_recv.at[z], cz_s, cz_r, ahead(off) * NQ + q).start()
    sum_recv[z] = sum_send[...]

    arrived(coef_all.at[pl.ds(0, NG - 1)], co_r)
    all_coef = jnp.concatenate(
        [coef_all[:, 0:8, :].reshape(64, 128), coef_all[:, 8:16, :].reshape(64, 128)], axis=0
    )[:, :EXPERTS]
    all_parts = jnp.concatenate(three_parts(all_coef), axis=1)
    for group in range(2):
        arrived(dp_recv.at[group, pl.ds(0, NG - 1)], da_r.at[group])
    crystals[...] = dp_recv[...].astype(F32).reshape(NZ * NG, 8, 128)
    flat = jnp.concatenate([crystals[:, row, :] for row in range(8)], axis=1).astype(BF16)
    terms = tn_dot(all_parts, flat)
    total = (terms[:EXPERTS] + terms[EXPERTS : 2 * EXPERTS] + terms[2 * EXPERTS :]).astype(BF16)
    for row in range(8):
        gather_send[row] = total[:, row * 128 : row * 128 + 128]
    for off in range(1, NG):
        dp_copy(gather_send, gather.at[pl.ds(h * 8, 8), x], ag_s, ag_r, (g + off) % NG).start()
    gather[pl.ds(h * 8, 8), x] = gather_send[...]

    for group in range(len(GROUPS)):
        forward_again(group)
    arrived(merged_send, fc_r)
    arrived(merged_send, gc_r)

    matrix = block[...].reshape(NZ * NQ * ROWS, COLS)
    f = feats[0]
    lifted = jnp.concatenate(
        [
            jnp.concatenate([f[:, :half], -f[:, half:]], axis=1),
            jnp.concatenate([f[:, half:], f[:, :half]], axis=1),
        ],
        axis=0,
    )
    messages = jnp.dot(lifted, matrix, preferred_element_type=F32).astype(BF16)
    messages = jnp.concatenate([messages[:EDGES], messages[EDGES:]], axis=1)
    node_rows[...] = jnp.dot(selector, messages, preferred_element_type=F32).astype(BF16)
    store_n = pltpu.make_async_copy(node_rows, node_out, out_sem.at[0])
    store_n.start()
    c = edge_cot[0]
    products = nt_dot(jnp.concatenate([c[:, :half], c[:, half:]], axis=0), matrix)
    grad_rows[:, :half] = (products[:EDGES, :half] + products[EDGES:, half:]).astype(BF16)
    grad_rows[:, half:] = (products[EDGES:, :half] - products[:EDGES, half:]).astype(BF16)
    store_e = pltpu.make_async_copy(grad_rows, edge_grad, out_sem.at[1])
    store_e.start()

    arrived(gather.at[pl.ds(0, 14)], ag_r)
    for row in range(ROWS):
        for tile in range(NX):
            weight_rows[:, pl.ds((row * NX + tile) * 128, 128)] = gather[row, tile]
    store_w = pltpu.make_async_copy(weight_rows, weight_out, out_sem.at[2])
    store_w.start()

    arrived(sum_recv.at[pl.ds(0, NZ - 1)], cz_r)
    summed = jnp.sum(sum_recv[...], axis=0)
    coef_out[...] = jnp.concatenate(
        [summed[a : a + 1, b * EXPERTS : (b + 1) * EXPERTS] for a in range(4) for b in range(4)], axis=0
    )

    sent(merged_send.at[pl.ds(0, NZ - 1)], fz_s)
    sent(merged_send, fy_s)
    sent(merged_send, fc_s)
    sent(merged_send, gc_s)
    sent(coef_all.at[pl.ds(0, NG - 1)], co_s)
    sent(z_send.at[pl.ds(0, NZ - 1)], bz_s)
    for group in range(2):
        sent(dp_send.at[group, pl.ds(0, NG - 1)], da_s.at[group])
    sent(gather.at[pl.ds(0, 14)], ag_s)
    sent(sum_recv.at[pl.ds(0, NZ - 1)], cz_s)
    feats_copy.wait_send()
    cot_copy.wait_send()
    core_part.wait_send()
    y_part.wait_send()
    for chunk in range(YC):
        ys(chunk).wait_send()
    store_n.wait()
    store_e.wait()
    store_w.wait()


def per_device(edge_feats, edge_dst, edge_live, coefficients, expert_weights, node_cot):
    vmem = pl.BlockSpec(memory_space=pltpu.VMEM)
    smem = pl.BlockSpec(memory_space=pltpu.SMEM)
    hbm = pl.BlockSpec(memory_space=pl.ANY)
    node_out, edge_grad, weight_grad, coef_grad = pl.pallas_call(
        kernel,
        out_shape=(
            jax.ShapeDtypeStruct((EDGES, WIDTH), BF16),
            jax.ShapeDtypeStruct((EDGES, WIDTH), BF16),
            jax.ShapeDtypeStruct((EXPERTS, ROWS * COLS), BF16),
            jax.ShapeDtypeStruct((NZ, EXPERTS), F32),
        ),
        in_specs=[hbm, hbm, smem, hbm, hbm, hbm],
        out_specs=(hbm, hbm, hbm, vmem),
        scratch_shapes=[
            pltpu.VMEM((EXPERTS, ROWS * COLS), F32),
            pltpu.VMEM((EXPERTS, ROWS * COLS), BF16),
            pltpu.VMEM((NZ, EXPERTS), F32),
            pltpu.VMEM((1, EDGES), jnp.int32),
            pltpu.VMEM((NZ, ROWS, COLS), F32),
            pltpu.VMEM((NZ, ROWS, COLS), BF16),
            pltpu.VMEM((NZ, NQ, ROWS, COLS), BF16),
            pltpu.VMEM((2, EDGES, WIDTH), BF16),
            pltpu.VMEM((EDGES, WIDTH), BF16),
            pltpu.VMEM((2, EDGES, WIDTH), BF16),
            pltpu.VMEM((NZ, 2, 2, ROWS, COLS), F32),
            pltpu.VMEM((NZ, ROWS, COLS), BF16),
            pltpu.VMEM((NZ, ROWS, COLS), BF16),
            pltpu.VMEM((NZ, ROWS, COLS), BF16),
            pltpu.VMEM((NZ, ROWS, COLS), BF16),
            pltpu.VMEM((NZ, ROWS, COLS), F32),
            pltpu.VMEM((2, NG, 4, 16, 128), BF16),
            pltpu.VMEM((2, NG, 4, 16, 128), BF16),
            pltpu.VMEM((NZ * NG, 8, 128), F32),
            pltpu.VMEM((ROWS, NX, EXPERTS, 128), BF16),
            pltpu.VMEM((8, EXPERTS, 128), BF16),
            pltpu.VMEM((NG, NZ, 128), F32),
            pltpu.VMEM((NZ, 128), F32),
            pltpu.VMEM((4, 4, 128), F32),
            pltpu.VMEM((4, 128), F32),
            pltpu.VMEM((NZ, 4, 128), F32),
            pltpu.VMEM((EDGES, WIDTH), BF16),
            pltpu.VMEM((EDGES, WIDTH), BF16),
            pltpu.VMEM((EXPERTS, ROWS * COLS), BF16),
            DMA((5,)), DMA((3,)),
            DMA, DMA((len(GROUPS),)), DMA, DMA((len(GROUPS),)), DMA, DMA, DMA, DMA,
            DMA((2,)), DMA((2,)), DMA, DMA,
            DMA((YC,)), DMA((YC,)), DMA, DMA((2,)), DMA((2,)), DMA((2,)),
            DMA, DMA, DMA, DMA, DMA((2,)), DMA((2,)),
        ],
        compiler_params=pltpu.CompilerParams(
            collective_id=0, has_side_effects=True, vmem_limit_bytes=60 * 1024 * 1024
        ),
    )(edge_feats, edge_dst.reshape(1, EDGES), edge_live, coefficients, expert_weights, node_cot)
    return node_out, edge_grad, weight_grad.astype(F32), coef_grad


def solution(mesh):
    in_specs = (
        P(("dp", "shard"), None),
        P(("dp", "shard")),
        P(("dp", "shard")),
        P("dp", None),
        P(None, "shard"),
        P(("dp", "shard"), None),
    )
    out_specs = (
        P(("dp", "shard"), None),
        P(("dp", "shard"), None),
        P(None, "shard"),
        P("dp", None),
    )
    return jax.shard_map(
        per_device, mesh=mesh, in_specs=in_specs, out_specs=out_specs, check_vma=False
    )
```

time: 381 us -> 62.1 us (0.16)
  the two profiles are of different devices: /device:TPU:1 before, /device:TPU:7 now
where the time goes in v2:
time: 62.1 us; the launch traced here: 61.9 us
  Pallas kernels  56.1 us (90%)
  local copies, waits for them, and re-layouts  2.35 us (4%)
  other arithmetic  2.12 us (3%)
  between operations  1.3 us (2%)
    pallas_call x1, Pallas kernels, per_device(): pl.pallas_call(kernel, out_shape=(jax.ShapeDtypeStruct((EDGES, WIDTH), BF...  56.1 us
    unnamed x9, local copies, waits for them, and re-layouts  2.35 us
    convert_element_type x1, other arithmetic, per_device(): return (node_out, edge_grad, weight_grad.astype(F32), coef_grad)  2.12 us

profile of v2, /device:TPU:7, one launch (start us, length us, event | category | flops | bytes accessed | tf_op | source)
XLA Modules:
  0.0 61.9 jit_solution(8713745352694393362)
XLA Ops:
  1.3 56.1 %shard_map.93 = (bf16[128,1024]{1,0:T(8,128)(2,1)}, bf16[128,1024]{1,0:T(8,128)(2,1)}, bf16[32,8192]{1,0:T(8,128)(2,1)}, f32[16,32]{1,0:T(8,128)}) custom-call(bf16[128,1024]{1,0:T(8,128)(2,1)} %feats_in.1, s32[1,128]{1,0:T(1,128)} %bitcast.1, s32[1]{0:T(128)S(6)} %copy.13.live_in, f32[16,32]{1,0:T(8,128)} %coef_in.1, f32[32,8192]{1,0:T(8,128)} %weights_in.1, ...), custom_call_target="tpu_custom_call" | custom-call | tf_op jit(solution)/shard_map/pallas_call | solution.py:323
  57.4 0.0 copy-start.1
  57.4 2.1 %convert_element_type.3 = f32[32,8192]{1,0:T(8,128)} convert(bf16[32,8192]{1,0:T(8,128)(2,1)} %get-tuple-element.10) | non-fusion elementwise | flops 262144 | bytes 1572864 | tf_op jit(solution)/shard_map/convert_element_type | solution.py:373
  59.5 0.0 copy-done.1
  59.5 0.0 copy-start
  59.5 0.7 %copy.14 = bf16[128,1024]{1,0:T(8,128)(2,1)} copy(bf16[128,1024]{1,0:T(8,128)(2,1)S(1)} %copy-done.1) | data formatting | bytes 524288
  60.2 0.3 copy-done
  60.6 0.0 copy-start.2
  60.6 0.7 %copy.15 = bf16[128,1024]{1,0:T(8,128)(2,1)} copy(bf16[128,1024]{1,0:T(8,128)(2,1)S(1)} %copy-done) | data formatting | bytes 524288
  61.3 0.0 copy-done.2
  61.3 0.6 copy.16
Async XLA Ops:
  57.4 2.1 %copy-start.1 = (bf16[128,1024]{1,0:T(8,128)(2,1)S(1)}, bf16[128,1024]{1,0:T(8,128)(2,1)}, u32[]{:S(2)}) copy-start(bf16[128,1024]{1,0:T(8,128)(2,1)} %get-tuple-element.16) | copy-start | bytes 786436
  59.5 1.0 %copy-start = (bf16[128,1024]{1,0:T(8,128)(2,1)S(1)}, bf16[128,1024]{1,0:T(8,128)(2,1)}, u32[]{:S(2)}) copy-start(bf16[128,1024]{1,0:T(8,128)(2,1)} %get-tuple-element.17) | copy-start | bytes 786436
  60.6 0.7 %copy-start.2 = (f32[16,32]{1,0:T(8,128)S(1)}, f32[16,32]{1,0:T(8,128)}, u32[]{:S(2)}) copy-start(f32[16,32]{1,0:T(8,128)} %get-tuple-element.19) | copy-start | bytes 6148

commit v3 on v2

--- a/solution.py
+++ b/solution.py
@@ -13,8 +13,11 @@
 YC = 4
 PER = NZ // YC
 OFFS = [8, 7, 9, 6, 10, 5, 11, 4, 12, 3, 13, 2, 14, 1, 15, 0]
-FAR = 5
-GROUPS = [[0, 8, 7, 9, 6, 10], [5, 11, 4, 12], [3, 13], [2, 14], [1, 15]]
+FIRST, SECOND, THIRD = [4, 12, 3, 13, 2, 14, 1, 15], [8, 7, 9], [6, 10, 5, 11]
+GROUPS = [[0, 4, 12, 3, 13, 2, 14, 1, 15], [8, 7, 9], [6, 10], [5, 11]]
+NEAR = [4, 12, 3, 13, 2, 14, 1, 15]
+PARTS = 4
+FINISH_LIMIT = 60
 GROUP_OF = {off: group for group, offs in enumerate(GROUPS) for off in offs}
 DMA = pltpu.SemaphoreType.DMA
 
@@ -41,9 +44,9 @@
     weights, copies, coef, dst, merged_rows, merged_send, block, feats, node_cot, edge_cot,
     grads, y_send, y_recv, z_send, z_recv, z_wide, dp_send, dp_recv, crystals, gather,
     gather_send, coef_all, planes, part, sum_send, sum_recv,
-    node_rows, grad_rows, weight_rows,
+    node_rows, grad_rows,
     in_sem, out_sem, fz_s, fz_r, fy_s, fy_r, fc_s, fc_r, gc_s, gc_r, ex_s, ex_r, co_s, co_r,
-    ys_s, ys_r, bz_s, bz_r, da_s, da_r, ag_s, ag_r, cz_s, cz_r, pt_s, pt_r,
+    ys_s, ys_r, bz_s, bz_r, da_s, da_r, ag_s, ag_r, ah_s, ah_r, cz_s, cz_r, pt_s, pt_r, far_sem,
 ):
     g = lax.axis_index("dp")
     s = lax.axis_index("shard")
@@ -99,7 +102,7 @@
             barrier, inc=1, device_id={"dp": dp, "shard": shard}, device_id_type=pl.DeviceIdType.MESH
         )
 
-    for off in OFFS[:-1]:
+    for off in NEAR:
         greet(g, ahead(off) * NQ + q)
     for off in range(1, NG):
         greet((g + off) % NG, s)
@@ -131,7 +134,11 @@
     edge_cot[0] = tn_dot(selector, node_cot[...]).astype(BF16)
     load_f.wait()
 
-    pl.semaphore_wait(barrier, 2 + (NZ - 1) + (NG - 1))
+    pl.semaphore_wait(barrier, 2 + len(NEAR) + (NG - 1))
+    for off in (4, NZ - 4):
+        pl.semaphore_signal(
+            far_sem, inc=1, device_id={"dp": g, "shard": ahead(off) * NQ + q}, device_id_type=pl.DeviceIdType.MESH
+        )
 
     feats_copy = shard_copy(feats.at[0], feats.at[1], ex_s.at[0], ex_r.at[0], core_peer)
     cot_copy = shard_copy(edge_cot.at[0], edge_cot.at[1], ex_s.at[1], ex_r.at[1], core_peer)
@@ -142,7 +149,7 @@
         to = ahead(off)
         return shard_copy(merged_send.at[to], block.at[z, q], fz_s, fz_r.at[GROUP_OF[off]], to * NQ + q)
 
-    for off in OFFS[:FAR]:
+    for off in FIRST:
         fz(off).start()
     for off in range(1, NG):
         dp_copy(coef_all.at[g], coef_all.at[g], co_s, co_r, (g + off) % NG).start()
@@ -170,6 +177,10 @@
             y_send[j] = grads[ahead(OFFS[j]), 1 - yh, core].astype(BF16)
         ys(chunk).start()
 
+    pl.semaphore_wait(far_sem, 2)
+    for off in SECOND:
+        fz(off).start()
+
     for chunk in range(YC):
         ys(chunk).wait_recv()
         for j in range(chunk * PER, chunk * PER + PER):
@@ -179,7 +190,7 @@
                 shard_copy(z_send.at[j], z_recv.at[j], bz_s, bz_r.at[j // 8], to * NQ + q).start()
     z_recv[NZ - 1] = z_send[NZ - 1]
 
-    for off in OFFS[FAR:-1]:
+    for off in THIRD:
         fz(off).start()
 
     def forward(group):
@@ -252,10 +263,17 @@
     total = (terms[:EXPERTS] + terms[EXPERTS : 2 * EXPERTS] + terms[2 * EXPERTS :]).astype(BF16)
     for row in range(8):
         gather_send[row] = total[:, row * 128 : row * 128 + 128]
-    for off in range(1, NG):
-        dp_copy(gather_send, gather.at[pl.ds(h * 8, 8), x], ag_s, ag_r, (g + off) % NG).start()
+    own_rows = pl.ds(h * 8, 8)
+    other_rows = pl.ds((1 - h) * 8, 8)
+    dp_copy(gather_send, gather.at[own_rows, x], ah_s, ah_r, (1 - h) * NX + x).start()
+    for off in (2, 1, 3):
+        dp_copy(gather_send, gather.at[own_rows, x], ag_s, ag_r, h * NX + (x + off) % NX).start()
     gather[pl.ds(h * 8, 8), x] = gather_send[...]
 
+    arrived(gather_send, ah_r)
+    relayed = gather.at[other_rows, x]
+    for off in (2, 1, 3):
+        dp_copy(relayed, relayed, ag_s, ag_r, h * NX + (x + off) % NX).start()
     for group in range(len(GROUPS)):
         forward_again(group)
     arrived(merged_send, fc_r)
@@ -282,11 +300,8 @@
     store_e = pltpu.make_async_copy(grad_rows, edge_grad, out_sem.at[1])
     store_e.start()
 
-    arrived(gather.at[pl.ds(0, 14)], ag_r)
-    for row in range(ROWS):
-        for tile in range(NX):
-            weight_rows[:, pl.ds((row * NX + tile) * 128, 128)] = gather[row, tile]
-    store_w = pltpu.make_async_copy(weight_rows, weight_out, out_sem.at[2])
+    arrived(gather.at[pl.ds(0, 12)], ag_r)
+    store_w = pltpu.make_async_copy(gather, weight_out, out_sem.at[2])
     store_w.start()
 
     arrived(sum_recv.at[pl.ds(0, NZ - 1)], cz_r)
@@ -303,7 +318,8 @@
     sent(z_send.at[pl.ds(0, NZ - 1)], bz_s)
     for group in range(2):
         sent(dp_send.at[group, pl.ds(0, NG - 1)], da_s.at[group])
-    sent(gather.at[pl.ds(0, 14)], ag_s)
+    sent(gather.at[pl.ds(0, 12)], ag_s)
+    sent(gather_send, ah_s)
     sent(sum_recv.at[pl.ds(0, NZ - 1)], cz_s)
     feats_copy.wait_send()
     cot_copy.wait_send()
@@ -316,16 +332,51 @@
     store_w.wait()
 
 
+def finish(
+    node_rows, grad_rows, gathered, coef_rows, node_out, edge_grad, weight_out, coef_out,
+    tiles, wide, node_held, grad_held, coef_held, sem, in_sem, out_sem,
+):
+    per = ROWS // PARTS
+    moves = [
+        (pltpu.make_async_copy(src, held, sem.at[n]), pltpu.make_async_copy(held, dst, sem.at[3 + n]))
+        for n, (src, held, dst) in enumerate(
+            ((node_rows, node_held, node_out), (grad_rows, grad_held, edge_grad), (coef_rows, coef_held, coef_out))
+        )
+    ]
+    loads = [
+        pltpu.make_async_copy(gathered.at[pl.ds(n * per, per)], tiles.at[pl.ds(n * per, per)], in_sem.at[n])
+        for n in range(PARTS)
+    ]
+    for load in loads:
+        load.start()
+    for load, _ in moves:
+        load.start()
+    stores = []
+    for n in range(PARTS):
+        loads[n].wait()
+        for row in range(n * per, n * per + per):
+            for tile in range(NX):
+                wide[:, pl.ds((row * NX + tile) * 128, 128)] = tiles[row, tile].astype(F32)
+        lanes = pl.ds(n * per * COLS, per * COLS)
+        stores.append(pltpu.make_async_copy(wide.at[:, lanes], weight_out.at[:, lanes], out_sem.at[n]))
+        stores[n].start()
+    for load, store in moves:
+        load.wait()
+        store.start()
+    for store in [store for _, store in moves] + stores:
+        store.wait()
+
+
 def per_device(edge_feats, edge_dst, edge_live, coefficients, expert_weights, node_cot):
     vmem = pl.BlockSpec(memory_space=pltpu.VMEM)
     smem = pl.BlockSpec(memory_space=pltpu.SMEM)
     hbm = pl.BlockSpec(memory_space=pl.ANY)
-    node_out, edge_grad, weight_grad, coef_grad = pl.pallas_call(
+    node_rows, grad_rows, gathered, coef_rows = pl.pallas_call(
         kernel,
         out_shape=(
             jax.ShapeDtypeStruct((EDGES, WIDTH), BF16),
             jax.ShapeDtypeStruct((EDGES, WIDTH), BF16),
-            jax.ShapeDtypeStruct((EXPERTS, ROWS * COLS), BF16),
+            jax.ShapeDtypeStruct((ROWS, NX, EXPERTS, 128), BF16),
             jax.ShapeDtypeStruct((NZ, EXPERTS), F32),
         ),
         in_specs=[hbm, hbm, smem, hbm, hbm, hbm],
@@ -359,18 +410,36 @@
             pltpu.VMEM((NZ, 4, 128), F32),
             pltpu.VMEM((EDGES, WIDTH), BF16),
             pltpu.VMEM((EDGES, WIDTH), BF16),
-            pltpu.VMEM((EXPERTS, ROWS * COLS), BF16),
             DMA((5,)), DMA((3,)),
             DMA, DMA((len(GROUPS),)), DMA, DMA((len(GROUPS),)), DMA, DMA, DMA, DMA,
             DMA((2,)), DMA((2,)), DMA, DMA,
             DMA((YC,)), DMA((YC,)), DMA, DMA((2,)), DMA((2,)), DMA((2,)),
-            DMA, DMA, DMA, DMA, DMA((2,)), DMA((2,)),
+            DMA, DMA, DMA, DMA, DMA, DMA, DMA((2,)), DMA((2,)), pltpu.SemaphoreType.REGULAR,
         ],
         compiler_params=pltpu.CompilerParams(
             collective_id=0, has_side_effects=True, vmem_limit_bytes=60 * 1024 * 1024
         ),
     )(edge_feats, edge_dst.reshape(1, EDGES), edge_live, coefficients, expert_weights, node_cot)
-    return node_out, edge_grad, weight_grad.astype(F32), coef_grad
+    return pl.pallas_call(
+        finish,
+        out_shape=(
+            jax.ShapeDtypeStruct((EDGES, WIDTH), BF16),
+            jax.ShapeDtypeStruct((EDGES, WIDTH), BF16),
+            jax.ShapeDtypeStruct((EXPERTS, ROWS * COLS), F32),
+            jax.ShapeDtypeStruct((NZ, EXPERTS), F32),
+        ),
+        in_specs=[hbm, hbm, hbm, hbm],
+        out_specs=(hbm, hbm, hbm, hbm),
+        scratch_shapes=[
+            pltpu.VMEM((ROWS, NX, EXPERTS, 128), BF16),
+            pltpu.VMEM((EXPERTS, ROWS * COLS), F32),
+            pltpu.VMEM((EDGES, WIDTH), BF16),
+            pltpu.VMEM((EDGES, WIDTH), BF16),
+            pltpu.VMEM((NZ, EXPERTS), F32),
+            DMA((6,)), DMA((PARTS,)), DMA((PARTS,)),
+        ],
+        compiler_params=pltpu.CompilerParams(vmem_limit_bytes=FINISH_LIMIT * 1024 * 1024),
+    )(node_rows, grad_rows, gathered, coef_rows)
 
 
 def solution(mesh):

time: 62.1 us -> 56.6 us (0.911)
  the two profiles are of different devices: /device:TPU:7 before, /device:TPU:1 now
where the time goes in v3:
time: 56.6 us; the launch traced here: 56.4 us
  Pallas kernels  55.1 us (97%)
  between operations  1.29 us (2%)
    pallas_call x1, Pallas kernels, per_device(): pl.pallas_call(kernel, out_shape=(jax.ShapeDtypeStruct((EDGES, WIDTH), BF...  52.8 us
    pallas_call x1, Pallas kernels, per_device(): pl.pallas_call(finish, out_shape=(jax.ShapeDtypeStruct((EDGES, WIDTH), BF...  2.26 us

profile of v3, /device:TPU:1, one launch (start us, length us, event | category | flops | bytes accessed | tf_op | source)
XLA Modules:
  0.0 56.4 jit_solution(6332186665466451754)
XLA Ops:
  1.3 52.8 %shard_map.93 = (bf16[128,1024]{1,0:T(8,128)(2,1)}, bf16[128,1024]{1,0:T(8,128)(2,1)}, bf16[16,4,32,128]{3,2,1,0:T(8,128)(2,1)}, f32[16,32]{1,0:T(8,128)}) custom-call(bf16[128,1024]{1,0:T(8,128)(2,1)} %feats_in.1, s32[1,128]{1,0:T(1,128)} %bitcast.1, s32[1]{0:T(128)S(6)} %copy.10.live_in, f32[16,32]{1,0:T(8,128)} %coef_in.1, f32[32,8192]{1,0:T(8,128)} %weights_in.1, ...), custom_call_target="tpu_custom_call" | custom-call | tf_op jit(solution)/shard_map/pallas_call | solution.py:374
  54.1 2.3 %shard_map.94 = (bf16[128,1024]{1,0:T(8,128)(2,1)}, bf16[128,1024]{1,0:T(8,128)(2,1)}, f32[32,8192]{1,0:T(8,128)}, f32[16,32]{1,0:T(8,128)}) custom-call(bf16[128,1024]{1,0:T(8,128)(2,1)} %get-tuple-element.8.node_rows, bf16[128,1024]{1,0:T(8,128)(2,1)} %get-tuple-element.9.grad_rows, bf16[16,4,32,128]{3,2,1,0:T(8,128)(2,1)} %get-tuple-element.10.gathered, ...), custom_call_target="tpu_custom_call" | custom-call | tf_op jit(solution)/shard_map/pallas_call | solution.py:423

commit v4 on v3

--- a/solution.py
+++ b/solution.py
@@ -42,11 +42,11 @@
     feats_in, dst_in, live_in, coef_in, weights_in, cot_in,
     node_out, edge_grad, weight_out, coef_out,
     weights, copies, coef, dst, merged_rows, merged_send, block, feats, node_cot, edge_cot,
-    grads, y_send, y_recv, z_send, z_recv, z_wide, dp_send, dp_recv, crystals, gather,
+    grads, y_send, y_recv, z_send, z_recv, z_wide, dp_send, dp_recv, crystals,
     gather_send, coef_all, planes, part, sum_send, sum_recv,
     node_rows, grad_rows,
     in_sem, out_sem, fz_s, fz_r, fy_s, fy_r, fc_s, fc_r, gc_s, gc_r, ex_s, ex_r, co_s, co_r,
-    ys_s, ys_r, bz_s, bz_r, da_s, da_r, ag_s, ag_r, ah_s, ah_r, cz_s, cz_r, pt_s, pt_r, far_sem,
+    ys_s, ys_r, bz_s, bz_r, da_s, da_r, ag_s, ag_r, cz_s, cz_r, pt_s, pt_r, far_sem,
 ):
     g = lax.axis_index("dp")
     s = lax.axis_index("shard")
@@ -68,7 +68,7 @@
     load_c = pltpu.make_async_copy(cot_in, node_cot, in_sem.at[2])
     load_k = pltpu.make_async_copy(coef_in, coef, in_sem.at[3])
     load_d = pltpu.make_async_copy(dst_in, dst, in_sem.at[4])
-    for load in (load_w, load_k, load_d, load_c, load_f):
+    for load in (load_d, load_c, load_f, load_k, load_w):
         load.start()
 
     def copy_to(src, dst, send, recv, dp, shard):
@@ -108,6 +108,26 @@
         greet((g + off) % NG, s)
     greet(g, core_peer)
     greet(g, y_peer)
+
+    load_d.wait()
+    atom = lax.broadcasted_iota(jnp.int32, (EDGES, EDGES), 0)
+    slot = lax.broadcasted_iota(jnp.int32, (EDGES, EDGES), 1)
+    chosen = (dst[...] == atom) & (slot < live_in[0])
+    selector = jnp.where(chosen, 1.0, 0.0).astype(BF16)
+    load_c.wait()
+    edge_cot[0] = tn_dot(selector, node_cot[...]).astype(BF16)
+    load_f.wait()
+
+    pl.semaphore_wait(barrier, 2 + len(NEAR) + (NG - 1))
+    for off in (4, NZ - 4):
+        pl.semaphore_signal(
+            far_sem, inc=1, device_id={"dp": g, "shard": ahead(off) * NQ + q}, device_id_type=pl.DeviceIdType.MESH
+        )
+
+    feats_copy = shard_copy(feats.at[0], feats.at[1], ex_s.at[0], ex_r.at[0], core_peer)
+    cot_copy = shard_copy(edge_cot.at[0], edge_cot.at[1], ex_s.at[1], ex_r.at[1], core_peer)
+    feats_copy.start()
+    cot_copy.start()
 
     load_k.wait()
     stacked = jnp.concatenate(three_parts(coef[...]), axis=0)
@@ -124,26 +144,6 @@
         merged_rows[:, row, :] = terms[0:NZ] + terms[NZ : 2 * NZ] + terms[2 * NZ : 3 * NZ]
     merged_send[...] = merged_rows[...].astype(BF16)
     block[z, q] = merged_send[z]
-
-    load_d.wait()
-    atom = lax.broadcasted_iota(jnp.int32, (EDGES, EDGES), 0)
-    slot = lax.broadcasted_iota(jnp.int32, (EDGES, EDGES), 1)
-    chosen = (dst[...] == atom) & (slot < live_in[0])
-    selector = jnp.where(chosen, 1.0, 0.0).astype(BF16)
-    load_c.wait()
-    edge_cot[0] = tn_dot(selector, node_cot[...]).astype(BF16)
-    load_f.wait()
-
-    pl.semaphore_wait(barrier, 2 + len(NEAR) + (NG - 1))
-    for off in (4, NZ - 4):
-        pl.semaphore_signal(
-            far_sem, inc=1, device_id={"dp": g, "shard": ahead(off) * NQ + q}, device_id_type=pl.DeviceIdType.MESH
-        )
-
-    feats_copy = shard_copy(feats.at[0], feats.at[1], ex_s.at[0], ex_r.at[0], core_peer)
-    cot_copy = shard_copy(edge_cot.at[0], edge_cot.at[1], ex_s.at[1], ex_r.at[1], core_peer)
-    feats_copy.start()
-    cot_copy.start()
 
     def fz(off):
         to = ahead(off)
@@ -227,7 +227,8 @@
             dp_copy(dp_send.at[group, to], dp_recv.at[group, g], da_s.at[group], da_r.at[group], to).start()
         dp_recv[group, g] = dp_send[group, g]
 
-    forward(0)
+    for group in range(2):
+        forward(group)
     arrived(z_recv.at[pl.ds(0, 8)], bz_r.at[0])
     own_slice(0)
     arrived(z_recv.at[pl.ds(0, 7)], bz_r.at[1])
@@ -241,15 +242,9 @@
     y_part = shard_copy(part.at[2], part.at[3], pt_s.at[1], pt_r.at[1], y_peer)
     y_part.start()
 
-    for group in range(1, len(GROUPS)):
-        forward(group)
-
-    y_part.wait_recv()
-    sum_send[...] = part[2] + part[3]
-    for off in OFFS[:-1]:
-        shard_copy(sum_send, sum_recv.at[z], cz_s, cz_r, ahead(off) * NQ + q).start()
-    sum_recv[z] = sum_send[...]
-
+    forward(2)
+
+    forward(3)
     arrived(coef_all.at[pl.ds(0, NG - 1)], co_r)
     all_coef = jnp.concatenate(
         [coef_all[:, 0:8, :].reshape(64, 128), coef_all[:, 8:16, :].reshape(64, 128)], axis=0
@@ -264,16 +259,17 @@
     for row in range(8):
         gather_send[row] = total[:, row * 128 : row * 128 + 128]
     own_rows = pl.ds(h * 8, 8)
-    other_rows = pl.ds((1 - h) * 8, 8)
-    dp_copy(gather_send, gather.at[own_rows, x], ah_s, ah_r, (1 - h) * NX + x).start()
-    for off in (2, 1, 3):
-        dp_copy(gather_send, gather.at[own_rows, x], ag_s, ag_r, h * NX + (x + off) % NX).start()
-    gather[pl.ds(h * 8, 8), x] = gather_send[...]
-
-    arrived(gather_send, ah_r)
-    relayed = gather.at[other_rows, x]
-    for off in (2, 1, 3):
-        dp_copy(relayed, relayed, ag_s, ag_r, h * NX + (x + off) % NX).start()
+    for off in (6, 2, 5, 7, 1, 3, 4):
+        dp_copy(gather_send, weight_out.at[own_rows, x], ag_s, ag_r, (g + off) % NG).start()
+    store_w = pltpu.make_async_copy(gather_send, weight_out.at[own_rows, x], out_sem.at[2])
+    store_w.start()
+
+    y_part.wait_recv()
+    sum_send[...] = part[2] + part[3]
+    for off in OFFS[:-1]:
+        shard_copy(sum_send, sum_recv.at[z], cz_s, cz_r, ahead(off) * NQ + q).start()
+    sum_recv[z] = sum_send[...]
+
     for group in range(len(GROUPS)):
         forward_again(group)
     arrived(merged_send, fc_r)
@@ -300,9 +296,7 @@
     store_e = pltpu.make_async_copy(grad_rows, edge_grad, out_sem.at[1])
     store_e.start()
 
-    arrived(gather.at[pl.ds(0, 12)], ag_r)
-    store_w = pltpu.make_async_copy(gather, weight_out, out_sem.at[2])
-    store_w.start()
+    arrived(weight_out.at[pl.ds(0, 14)], ag_r)
 
     arrived(sum_recv.at[pl.ds(0, NZ - 1)], cz_r)
     summed = jnp.sum(sum_recv[...], axis=0)
@@ -318,8 +312,7 @@
     sent(z_send.at[pl.ds(0, NZ - 1)], bz_s)
     for group in range(2):
         sent(dp_send.at[group, pl.ds(0, NG - 1)], da_s.at[group])
-    sent(gather.at[pl.ds(0, 12)], ag_s)
-    sent(gather_send, ah_s)
+    sent(weight_out.at[pl.ds(0, 14)], ag_s)
     sent(sum_recv.at[pl.ds(0, NZ - 1)], cz_s)
     feats_copy.wait_send()
     cot_copy.wait_send()
@@ -401,7 +394,6 @@
             pltpu.VMEM((2, NG, 4, 16, 128), BF16),
             pltpu.VMEM((2, NG, 4, 16, 128), BF16),
             pltpu.VMEM((NZ * NG, 8, 128), F32),
-            pltpu.VMEM((ROWS, NX, EXPERTS, 128), BF16),
             pltpu.VMEM((8, EXPERTS, 128), BF16),
             pltpu.VMEM((NG, NZ, 128), F32),
             pltpu.VMEM((NZ, 128), F32),
@@ -414,7 +406,7 @@
             DMA, DMA((len(GROUPS),)), DMA, DMA((len(GROUPS),)), DMA, DMA, DMA, DMA,
             DMA((2,)), DMA((2,)), DMA, DMA,
             DMA((YC,)), DMA((YC,)), DMA, DMA((2,)), DMA((2,)), DMA((2,)),
-            DMA, DMA, DMA, DMA, DMA, DMA, DMA((2,)), DMA((2,)), pltpu.SemaphoreType.REGULAR,
+            DMA, DMA, DMA, DMA, DMA((2,)), DMA((2,)), pltpu.SemaphoreType.REGULAR,
         ],
         compiler_params=pltpu.CompilerParams(
             collective_id=0, has_side_effects=True, vmem_limit_bytes=60 * 1024 * 1024

time: 56.6 us -> 56.2 us (level)
  no operation moved by 1% of the time
where the time goes in v4:
time: 56.2 us; the launch traced here: 56 us
  Pallas kernels  54.7 us (97%)
  between operations  1.29 us (2%)
    pallas_call x1, Pallas kernels, per_device(): pl.pallas_call(kernel, out_shape=(jax.ShapeDtypeStruct((EDGES, WIDTH), BF...  52.4 us
    pallas_call x1, Pallas kernels, per_device(): pl.pallas_call(finish, out_shape=(jax.ShapeDtypeStruct((EDGES, WIDTH), BF...  2.26 us

profile of v4, /device:TPU:1, one launch (start us, length us, event | category | flops | bytes accessed | tf_op | source)
XLA Modules:
  0.0 56.0 jit_solution(4338705466197485639)
XLA Ops:
  1.3 52.4 %shard_map.93 = (bf16[128,1024]{1,0:T(8,128)(2,1)}, bf16[128,1024]{1,0:T(8,128)(2,1)}, bf16[16,4,32,128]{3,2,1,0:T(8,128)(2,1)}, f32[16,32]{1,0:T(8,128)}) custom-call(bf16[128,1024]{1,0:T(8,128)(2,1)} %feats_in.1, s32[1,128]{1,0:T(1,128)} %bitcast.1, s32[1]{0:T(128)S(6)} %copy.10.live_in, f32[16,32]{1,0:T(8,128)} %coef_in.1, f32[32,8192]{1,0:T(8,128)} %weights_in.1, ...), custom_call_target="tpu_custom_call" | custom-call | tf_op jit(solution)/shard_map/pallas_call | solution.py:367
  53.7 2.3 %shard_map.94 = (bf16[128,1024]{1,0:T(8,128)(2,1)}, bf16[128,1024]{1,0:T(8,128)(2,1)}, f32[32,8192]{1,0:T(8,128)}, f32[16,32]{1,0:T(8,128)}) custom-call(bf16[128,1024]{1,0:T(8,128)(2,1)} %get-tuple-element.8.node_rows, bf16[128,1024]{1,0:T(8,128)(2,1)} %get-tuple-element.9.grad_rows, bf16[16,4,32,128]{3,2,1,0:T(8,128)(2,1)} %get-tuple-element.10.gathered, ...), custom_call_target="tpu_custom_call" | custom-call | tf_op jit(solution)/shard_map/pallas_call | solution.py:415

commit v5 on v4

--- a/solution.py
+++ b/solution.py
@@ -10,11 +10,11 @@
 NX = 4
 ROWS, COLS = 16, 512
 EDGES, WIDTH, EXPERTS = 128, 1024, 32
-YC = 4
+YC = 8
 PER = NZ // YC
 OFFS = [8, 7, 9, 6, 10, 5, 11, 4, 12, 3, 13, 2, 14, 1, 15, 0]
-FIRST, SECOND, THIRD = [4, 12, 3, 13, 2, 14, 1, 15], [8, 7, 9], [6, 10, 5, 11]
-GROUPS = [[0, 4, 12, 3, 13, 2, 14, 1, 15], [8, 7, 9], [6, 10], [5, 11]]
+FIRST, SECOND, THIRD = [4, 12, 3, 13, 2, 14, 1, 15], [8, 7, 9], [5, 11, 6, 10]
+GROUPS = [[0, 4, 12, 3, 13, 2, 14, 1, 15], [8, 7, 9], [5, 11], [6, 10]]
 NEAR = [4, 12, 3, 13, 2, 14, 1, 15]
 PARTS = 4
 FINISH_LIMIT = 60
@@ -210,11 +210,6 @@
     def own_slice(group):
         slots = slice(group * 8, group * 8 + 8)
         wide = z_recv[slots].astype(F32)
-        z_wide[slots] = wide
-        flat = jnp.concatenate([z_wide[slots, row, :] for row in range(ROWS)], axis=1).astype(BF16)
-        found = nt_dot(flat, copies[...])
-        for j in range(8):
-            planes[pl.ds(behind(OFFS[group * 8 + j]), 1), :] = jnp.concatenate([found[j : j + 1], blank], axis=1)
         for to in range(NG):
             rows = slice((to // NX) * 8, (to // NX) * 8 + 8)
             lanes = slice((to % NX) * 128, (to % NX) * 128 + 128)
@@ -226,6 +221,11 @@
             to = (g + off) % NG
             dp_copy(dp_send.at[group, to], dp_recv.at[group, g], da_s.at[group], da_r.at[group], to).start()
         dp_recv[group, g] = dp_send[group, g]
+        z_wide[slots] = wide
+        flat = jnp.concatenate([z_wide[slots, row, :] for row in range(ROWS)], axis=1).astype(BF16)
+        found = nt_dot(flat, copies[...])
+        for j in range(8):
+            planes[pl.ds(behind(OFFS[group * 8 + j]), 1), :] = jnp.concatenate([found[j : j + 1], blank], axis=1)
 
     for group in range(2):
         forward(group)

time: 56.2 us -> 54.6 us (0.972)
  Pallas kernels: 54.7 us -> 52.9 us
    pallas_call x1, Pallas kernels: 52.4 us -> 50.6 us  [per_device(): pl.pallas_call(kernel, out_shape=(jax.ShapeDtypeStruct((EDGES, WIDTH), BF...]
where the time goes in v5:
time: 54.6 us; the launch traced here: 54.2 us
  Pallas kernels  52.9 us (97%)
  between operations  1.29 us (2%)
    pallas_call x1, Pallas kernels, per_device(): pl.pallas_call(kernel, out_shape=(jax.ShapeDtypeStruct((EDGES, WIDTH), BF...  50.6 us
    pallas_call x1, Pallas kernels, per_device(): pl.pallas_call(finish, out_shape=(jax.ShapeDtypeStruct((EDGES, WIDTH), BF...  2.26 us

profile of v5, /device:TPU:1, one launch (start us, length us, event | category | flops | bytes accessed | tf_op | source)
XLA Modules:
  0.0 54.2 jit_solution(5971797479391528358)
XLA Ops:
  1.3 50.6 %shard_map.93 = (bf16[128,1024]{1,0:T(8,128)(2,1)}, bf16[128,1024]{1,0:T(8,128)(2,1)}, bf16[16,4,32,128]{3,2,1,0:T(8,128)(2,1)}, f32[16,32]{1,0:T(8,128)}) custom-call(bf16[128,1024]{1,0:T(8,128)(2,1)} %feats_in.1, s32[1,128]{1,0:T(1,128)} %bitcast.1, s32[1]{0:T(128)S(6)} %copy.10.live_in, f32[16,32]{1,0:T(8,128)} %coef_in.1, f32[32,8192]{1,0:T(8,128)} %weights_in.1, ...), custom_call_target="tpu_custom_call" | custom-call | tf_op jit(solution)/shard_map/pallas_call | solution.py:367
  51.9 2.3 %shard_map.94 = (bf16[128,1024]{1,0:T(8,128)(2,1)}, bf16[128,1024]{1,0:T(8,128)(2,1)}, f32[32,8192]{1,0:T(8,128)}, f32[16,32]{1,0:T(8,128)}) custom-call(bf16[128,1024]{1,0:T(8,128)(2,1)} %get-tuple-element.8.node_rows, bf16[128,1024]{1,0:T(8,128)(2,1)} %get-tuple-element.9.grad_rows, bf16[16,4,32,128]{3,2,1,0:T(8,128)(2,1)} %get-tuple-element.10.gathered, ...), custom_call_target="tpu_custom_call" | custom-call | tf_op jit(solution)/shard_map/pallas_call | solution.py:415
